TPU v7x, 32 devices: a whole 2x2x4 slice. The times are simulated.
32 devices in a mesh: dp: 2 (over x), ctx: 16 (over z, y, core).
Axes of the slice: x: 2, y: 2, z: 4, core: 2. Of those that a mesh axis runs over, the one named last changes fastest.
Arguments:
- grad_output: bfloat16 [2, 2048, 2048], P('dp', 'ctx'), may hold values from -0.125 to 0.125
- conv_input: bfloat16 [2, 2048, 2048], P('dp', 'ctx'), may hold values from -6 to 6
- filter_taps: bfloat16 [2048, 2048], P('ctx'), may hold values from -4 to 4
Outputs:
- grad_input: bfloat16 [2, 2048, 2048], P('dp', 'ctx')
- filter_grad: float32 [2048, 2048], P('ctx', 'dp')
All inputs are finite; a program needn't handle non-finite values.
Results may differ from a plain program's by a relative error of at most 0.001.
Values may be sent and summed in bfloat16 or wider, within the bound.
A program may use at most 64 MiB of HBM per device.

v0:
```python
import functools
import math

import jax
import jax.numpy as jnp
import numpy as np
from jax import lax
from jax.experimental import pallas as pl
from jax.experimental.pallas import tpu as pltpu
from jax.sharding import PartitionSpec as P


def angle_table(rows, cols, period):
    product = (
        lax.broadcasted_iota(jnp.int32, (rows, cols), 0)
        * lax.broadcasted_iota(jnp.int32, (rows, cols), 1)
        % period
    )
    phase = product.astype(jnp.float32) * (2.0 * math.pi / period)
    return (jnp.cos(phase), jnp.sin(phase))


def forward(values):
    blocks = values.shape[-2]
    tokens = values.shape[-1]
    rows = 2 * blocks
    block_cos, block_sin = angle_table(rows, blocks, rows)
    twist_cos, twist_sin = angle_table(rows, tokens, rows * tokens)
    inner_cos, inner_sin = angle_table(tokens, tokens, tokens)
    block_table = jnp.stack([block_cos, -block_sin])
    first = jnp.einsum("...qj,prq->...prj", values, block_table, precision=lax.Precision.HIGHEST)
    first_re = first[..., 0, :, :]
    first_im = first[..., 1, :, :]
    turned = jnp.stack(
        [first_re * twist_cos + first_im * twist_sin, first_im * twist_cos - first_re * twist_sin],
        axis=-3,
    )
    inner_table = jnp.stack([jnp.stack([inner_cos, -inner_sin]), jnp.stack([inner_sin, inner_cos])])
    return jnp.einsum("...prj,pojm->...orm", turned, inner_table, precision=lax.Precision.HIGHEST)


def inverse(spectrum):
    rows = spectrum.shape[-2]
    tokens = spectrum.shape[-1]
    blocks = rows // 2
    block_cos, block_sin = angle_table(rows, blocks, rows)
    twist_cos, twist_sin = angle_table(rows, tokens, rows * tokens)
    inner_cos, inner_sin = angle_table(tokens, tokens, tokens)
    inner_table = jnp.stack([jnp.stack([inner_cos, inner_sin]), jnp.stack([-inner_sin, inner_cos])])
    back = jnp.einsum("...prm,pomj->...orj", spectrum, inner_table, precision=lax.Precision.HIGHEST)
    back_re = back[..., 0, :, :]
    back_im = back[..., 1, :, :]
    turned = jnp.stack(
        [back_re * twist_cos - back_im * twist_sin, back_im * twist_cos + back_re * twist_sin],
        axis=-3,
    )
    block_table = jnp.stack([block_cos, -block_sin])
    result = jnp.einsum("...prj,prq->...qj", turned, block_table, precision=lax.Precision.HIGHEST)
    return result / (rows * tokens)


def conj_product(left, right):
    left_re = left[:, 0]
    left_im = left[:, 1]
    right_re = right[:, 0]
    right_im = right[:, 1]
    return jnp.stack(
        [left_re * right_re + left_im * right_im, left_im * right_re - left_re * right_im], axis=1
    )


def local(grad_output, conv_input, filter_taps):
    tokens = grad_output.shape[1]
    width = grad_output.shape[2]
    groups = lax.axis_size("ctx")
    group_width = width // groups

    def to_groups(values):
        return jnp.transpose(values.reshape(tokens, groups, group_width), (1, 2, 0))[:, :, None, :]

    grad_cols, input_cols, taps_cols = (
        lax.all_to_all(to_groups(grad_output[0]), "ctx", split_axis=0, concat_axis=2, tiled=True),
        lax.all_to_all(to_groups(conv_input[0]), "ctx", split_axis=0, concat_axis=2, tiled=True),
        lax.all_to_all(to_groups(filter_taps), "ctx", split_axis=0, concat_axis=2, tiled=True),
    )
    filter_spec = forward(taps_cols[0].astype(jnp.float32))
    stacked = jnp.stack([grad_cols[0], input_cols[0]]).astype(jnp.float32)
    spectra = forward(stacked)
    grad_spec = spectra[0]
    input_spec = spectra[1]
    cross = conj_product(grad_spec, filter_spec)
    corr = conj_product(grad_spec, input_spec)
    results = inverse(jnp.stack([cross, corr]))
    grad_cols_out = results[0]
    filter_part = lax.psum_scatter(results[1], "dp", scatter_dimension=1, tiled=True)
    filter_grad = filter_part.reshape(group_width, -1)
    rounded = grad_cols_out.astype(jnp.bfloat16)[None]
    returned = lax.all_to_all(rounded, "ctx", split_axis=2, concat_axis=0, tiled=True)
    grad_input = jnp.transpose(returned[:, :, 0, :], (2, 0, 1)).reshape(tokens, width)[None]
    return (grad_input, filter_grad)


INNER = 256
RADIX = 16
HALF = RADIX // 2
KEPT = HALF + 1
LANES = 128
ROWS = 16
MESH = pl.DeviceIdType.MESH


def inner_tables():
    index = np.arange(INNER)
    phase = 2.0 * np.pi * (np.outer(index, index) % INNER) / INNER
    cos, sin = np.cos(phase), np.sin(phase)
    table = np.block([[cos, sin], [-sin, cos]]).astype(np.float32)
    high = table.astype(jnp.bfloat16)
    low = (table - high.astype(np.float32)).astype(jnp.bfloat16)
    return np.stack([high, low])


def twist_columns():
    phase = 2.0 * np.pi * np.outer(np.arange(INNER), np.arange(1, KEPT)) / (RADIX * INNER)
    columns = np.zeros((INNER, LANES), np.float32)
    columns[:, :HALF] = np.cos(phase)
    columns[:, HALF : 2 * HALF] = np.sin(phase)
    return columns


def cmul(a, c, s):
    return (a[0] * c - a[1] * s, a[0] * s + a[1] * c)


def cadd(a, b):
    return (a[0] + b[0], a[1] + b[1])


def csub(a, b):
    return (a[0] - b[0], a[1] - b[1])


def times_i(a):
    return (-a[1], a[0])


def spread(x):
    s = math.sqrt(0.5)
    a = [x[q] + x[q + 4] for q in range(4)]
    b = [x[q] - x[q + 4] for q in range(4)]
    out = [None] * KEPT
    out[0] = (a[0] + a[2]) + (a[1] + a[3])
    out[8] = (a[0] + a[2]) - (a[1] + a[3])
    out[4] = (a[0] - a[2], a[3] - a[1])
    diff, both = s * (b[1] - b[3]), s * (b[1] + b[3])
    out[2] = (b[0] + diff, -b[2] - both)
    out[6] = (b[0] - diff, b[2] - both)
    u = [(x[0], -x[4])]
    for q in range(1, 4):
        c, t = math.cos(2.0 * math.pi * q / RADIX), math.sin(2.0 * math.pi * q / RADIX)
        u.append((x[q] * c - x[q + 4] * t, -(x[q + 4] * c + x[q] * t)))
    e0, e1 = cadd(u[0], u[2]), csub(u[0], u[2])
    f0, f1 = cadd(u[1], u[3]), times_i(csub(u[1], u[3]))
    out[1] = cadd(e0, f0)
    out[5] = csub(e1, f1)
    v2, v3 = csub(e0, f0), cadd(e1, f1)
    out[7] = (v2[0], -v2[1])
    out[3] = (v3[0], -v3[1])
    return out


def gather(z):
    s = math.sqrt(0.5)
    total, diff = z[0] + z[8], z[0] - z[8]
    plus, minus = total + z[4][0], total - z[4][0]
    sr, si = z[2][0] + z[6][0], z[6][1] - z[2][1]
    p = (s * (z[2][0] - z[2][1]), s * (z[2][0] + z[2][1]))
    w = (-s * (z[6][0] + z[6][1]), s * (z[6][0] - z[6][1]))
    pw, wp = p[0] + w[0], w[1] - p[1]
    down, up = diff - z[4][1], diff + z[4][1]
    even = [plus + sr, down + pw, minus + si, up + wp, plus - sr, down - pw, minus - si, up - wp]
    v = [z[1], z[5], (z[7][0], -z[7][1]), (z[3][0], -z[3][1])]
    e0, e1 = cadd(v[0], v[2]), csub(v[0], v[2])
    f0, f1 = cadd(v[1], v[3]), times_i(csub(v[1], v[3]))
    u = [cadd(e0, f0), cadd(e1, f1), csub(e0, f0), csub(e1, f1)]
    out = [None] * HALF
    for q in range(4):
        o = cmul(u[q], math.cos(2.0 * math.pi * q / RADIX), math.sin(2.0 * math.pi * q / RADIX))
        out[q] = even[q] + o[0]
        out[q + 4] = even[q + 4] - o[1]
    return out


def put_parts(high_ref, low_ref, row, r, value):
    high = value.astype(jnp.bfloat16)
    at = (pl.ds(pl.multiple_of(row, ROWS), ROWS), pl.ds(r * LANES, LANES))
    high_ref[at] = high
    low_ref[at] = (value - high.astype(jnp.float32)).astype(jnp.bfloat16)


def inner_dft(table_ref, high_ref, low_ref, out_ref):
    def block(at):
        high, low = high_ref[:, at], low_ref[:, at]
        out_ref[:, at] = (
            jnp.dot(table_ref[0], high, preferred_element_type=jnp.float32)
            + jnp.dot(table_ref[0], low, preferred_element_type=jnp.float32)
            + jnp.dot(table_ref[1], high, preferred_element_type=jnp.float32)
        )

    @pl.loop(0, HALF // 2)
    def _(i):
        block(pl.ds(pl.multiple_of(i * 2 * LANES, 2 * LANES), 2 * LANES))

    block(pl.ds(HALF * LANES, LANES))


def transform(source_ref, twist_ref, table_ref, high_ref, low_ref, spec_ref):
    @pl.loop(0, INNER // ROWS)
    def _(i):
        row = i * ROWS
        rows = pl.ds(pl.multiple_of(row, ROWS), ROWS)
        x = [
            source_ref[pl.ds(pl.multiple_of(q * INNER + row, ROWS), ROWS), :].astype(jnp.float32)
            for q in range(HALF)
        ]
        out = spread(x)
        put_parts(high_ref, low_ref, row, 0, out[0])
        put_parts(high_ref, low_ref, INNER + row, 0, jnp.zeros_like(out[0]))
        out[8] = (out[8], None)
        for r in range(1, KEPT):
            c, s = twist_ref[r - 1, rows, :], twist_ref[HALF + r - 1, rows, :]
            re, im = out[r]
            if im is None:
                re, im = re * c, -(re * s)
            else:
                re, im = re * c + im * s, im * c - re * s
            put_parts(high_ref, low_ref, row, r, re)
            put_parts(high_ref, low_ref, INNER + row, r, im)

    inner_dft(table_ref, high_ref, low_ref, spec_ref)


def correlate(left_ref, right_ref, twist_ref, table_ref, high_ref, low_ref, work_ref, store):
    @pl.loop(0, INNER // ROWS)
    def _(i):
        row = i * ROWS
        top = pl.ds(pl.multiple_of(row, ROWS), ROWS)
        bottom = pl.ds(pl.multiple_of(INNER + row, ROWS), ROWS)
        for r in range(KEPT):
            lanes = pl.ds(r * LANES, LANES)
            scale = (1.0 if r in (0, HALF) else 2.0) / (RADIX * INNER)
            lr, li = left_ref[top, lanes] * scale, left_ref[bottom, lanes] * scale
            rr, ri = right_ref[top, lanes], right_ref[bottom, lanes]
            put_parts(high_ref, low_ref, row, r, li * rr - lr * ri)
            put_parts(high_ref, low_ref, INNER + row, r, lr * rr + li * ri)

    inner_dft(table_ref, high_ref, low_ref, work_ref)

    @pl.loop(0, INNER // ROWS)
    def _(i):
        row = i * ROWS
        top = pl.ds(pl.multiple_of(row, ROWS), ROWS)
        bottom = pl.ds(pl.multiple_of(INNER + row, ROWS), ROWS)
        z = [work_ref[bottom, pl.ds(0, LANES)]]
        for r in range(1, KEPT):
            lanes = pl.ds(r * LANES, LANES)
            im, re = work_ref[top, lanes], work_ref[bottom, lanes]
            c, s = twist_ref[r - 1, top, :], twist_ref[HALF + r - 1, top, :]
            z.append((re * c - im * s, re * s + im * c))
        z[8] = z[8][0]
        for q, value in enumerate(gather(z)):
            store(q * INNER + row, value)


def kernel(
    groups,
    grad_ref,
    input_ref,
    taps_ref,
    table_ref,
    columns_ref,
    grad_input_ref,
    filter_grad_ref,
    grad_in,
    taps_in,
    input_in,
    grad_spec,
    taps_spec,
    input_spec,
    work,
    high,
    low,
    twist,
    back,
    partial,
    arrived,
    send_sem,
    recv_sem,
    own_sem,
    pair_send,
    pair_recv,
):
    tokens = grad_ref.shape[0]
    half = partial.shape[0] // 2
    me = lax.axis_index("ctx")
    group = lax.axis_index("dp")
    other = 1 - group

    barrier = pltpu.get_barrier_semaphore()

    @pl.loop(1, groups)
    def _(d):
        pl.semaphore_signal(
            barrier, inc=1, device_id=(group, lax.rem(me + d, groups)), device_id_type=MESH
        )

    pl.semaphore_signal(barrier, inc=1, device_id=(other, me), device_id_type=MESH)
    pl.semaphore_wait(barrier, groups)

    def rows_of(device):
        return pl.ds(pl.multiple_of(device * tokens, tokens), tokens)

    def lanes_of(device):
        return pl.ds(pl.multiple_of(device * LANES, LANES), LANES)

    outward = ((grad_ref, grad_in), (taps_ref, taps_in), (input_ref, input_in))

    def copy_out(a, peer, dest_rows, recv_at):
        source, landing = outward[a]
        return pltpu.make_async_remote_copy(
            src_ref=source.at[:, lanes_of(peer)],
            dst_ref=landing.at[rows_of(dest_rows), :],
            send_sem=send_sem.at[a, peer],
            recv_sem=recv_sem.at[a, recv_at],
            device_id=(group, peer),
            device_id_type=MESH,
        )

    def copy_back(peer, dest_lanes, recv_at):
        return pltpu.make_async_remote_copy(
            src_ref=back.at[rows_of(peer), :],
            dst_ref=grad_input_ref.at[:, lanes_of(dest_lanes)],
            send_sem=send_sem.at[3, peer],
            recv_sem=recv_sem.at[3, recv_at],
            device_id=(group, peer),
            device_id_type=MESH,
        )

    def own_out(a):
        source, landing = outward[a]
        return pltpu.make_async_copy(
            source.at[:, lanes_of(me)], landing.at[rows_of(me), :], own_sem.at[a]
        )

    def own_back():
        return pltpu.make_async_copy(
            back.at[rows_of(me), :], grad_input_ref.at[:, lanes_of(me)], own_sem.at[3]
        )

    for a in range(3):

        @pl.loop(1, groups)
        def _(d):
            copy_out(a, lax.rem(me + d, groups), me, me).start()

        own_out(a).start()

    for i in range(2 * HALF):
        twist[i] = jnp.broadcast_to(columns_ref[:, i : i + 1], (INNER, LANES))

    def wait_for(a):
        own_out(a).wait()

        @pl.loop(1, groups)
        def _(d):
            peer = lax.rem(me + d, groups)
            copy_out(a, peer, peer, peer).wait_recv()

    shared = (twist, table_ref, high, low)
    wait_for(0)
    transform(grad_in, *shared, grad_spec)
    wait_for(1)
    transform(taps_in, *shared, taps_spec)

    def store_back(row, value):
        back[pl.ds(pl.multiple_of(row, ROWS), ROWS), :] = value.astype(jnp.bfloat16)

    correlate(grad_spec, taps_spec, *shared, work, store_back)

    @pl.loop(1, groups)
    def _(d):
        copy_back(lax.rem(me + d, groups), me, me).start()

    own_back().start()
    wait_for(2)
    transform(input_in, *shared, input_spec)

    def store_partial(row, value):
        partial[pl.ds(pl.multiple_of(row, ROWS), ROWS), :] = value

    correlate(grad_spec, input_spec, *shared, work, store_partial)
    pair = pltpu.make_async_remote_copy(
        src_ref=partial.at[pl.ds(pl.multiple_of(other * half, half), half), :],
        dst_ref=arrived,
        send_sem=pair_send,
        recv_sem=pair_recv,
        device_id=(other, me),
        device_id_type=MESH,
    )
    pair.start()
    pair.wait()

    for i in range(half // LANES):
        mine = partial[pl.ds(pl.multiple_of(group * half + i * LANES, LANES), LANES), :]
        filter_grad_ref[:, i * LANES : (i + 1) * LANES] = jnp.transpose(
            mine + arrived[i * LANES : (i + 1) * LANES, :]
        )

    own_back().wait()

    @pl.loop(1, groups)
    def _(d):
        peer = lax.rem(me + d, groups)
        copy_back(peer, peer, peer).wait()
        for a in range(3):
            copy_out(a, peer, peer, peer).wait_send()


def fused(grad_output, conv_input, filter_taps):
    groups = lax.axis_size("ctx")
    tokens, width = filter_taps.shape
    length = groups * tokens
    anywhere = pl.BlockSpec(memory_space=pl.ANY)
    vmem = pl.BlockSpec(memory_space=pltpu.VMEM)
    landing = pltpu.VMEM((length, LANES), jnp.bfloat16)
    spec = pltpu.VMEM((2 * INNER, KEPT * LANES), jnp.float32)
    part = pltpu.VMEM((2 * INNER, KEPT * LANES), jnp.bfloat16)
    grad_input, filter_grad = pl.pallas_call(
        functools.partial(kernel, groups),
        out_shape=(
            jax.ShapeDtypeStruct((tokens, width), jnp.bfloat16),
            jax.ShapeDtypeStruct((LANES, length // 2), jnp.float32),
        ),
        in_specs=[anywhere, anywhere, anywhere, vmem, vmem],
        out_specs=(anywhere, vmem),
        scratch_shapes=[
            landing,
            landing,
            landing,
            spec,
            spec,
            spec,
            spec,
            part,
            part,
            pltpu.VMEM((2 * HALF, INNER, LANES), jnp.float32),
            pltpu.VMEM((length, LANES), jnp.bfloat16),
            pltpu.VMEM((length, LANES), jnp.float32),
            pltpu.VMEM((length // 2, LANES), jnp.float32),
            pltpu.SemaphoreType.DMA((4, groups)),
            pltpu.SemaphoreType.DMA((4, groups)),
            pltpu.SemaphoreType.DMA((4,)),
            pltpu.SemaphoreType.DMA,
            pltpu.SemaphoreType.DMA,
        ],
        compiler_params=pltpu.CompilerParams(
            collective_id=0, has_side_effects=True, vmem_limit_bytes=40 * 1024 * 1024
        ),
        cost_estimate=pl.CostEstimate(
            flops=5 * 3 * 2 * 512 * 512 * KEPT * LANES, bytes_accessed=6 << 20, transcendentals=0
        ),
    )(
        grad_output[0],
        conv_input[0],
        filter_taps,
        jnp.asarray(inner_tables()),
        jnp.asarray(twist_columns()),
    )
    return (grad_input[None], filter_grad)


def any_size(grad_output, conv_input, filter_taps):
    groups = lax.axis_size("ctx")
    tokens, width = filter_taps.shape
    fits = (
        lax.axis_size("dp") == 2
        and groups * tokens == HALF * INNER
        and width == groups * LANES
        and tokens % ROWS == 0
    )
    return (fused if fits else local)(grad_output, conv_input, filter_taps)


def solution(mesh):
    placed = (P("dp", "ctx", None), P("dp", "ctx", None), P("ctx", None))
    return jax.shard_map(
        any_size,
        mesh=mesh,
        in_specs=placed,
        out_specs=(P("dp", "ctx", None), P("ctx", "dp")),
        check_vma=False,
    )
```

profile of v0, /device:TPU:29, one launch (start us, length us, event | category | flops | bytes accessed | tf_op | source)
XLA Modules:
  0.0 72.9 jit_solution(9114623162399751550)
XLA Ops:
  0.6 0.0 copy-start
  0.6 1.0 %copy-done = bf16[1,128,2048]{2,1,0:T(8,128)(2,1)S(1)} copy-done((bf16[1,128,2048]{2,1,0:T(8,128)(2,1)S(1)}, bf16[1,128,2048]{2,1,0:T(8,128)(2,1)}, u32[]{:S(2)}) %copy-start) | copy-done | bytes 524312
  1.7 0.0 copy-start.1
  1.7 1.0 %copy-done.1 = bf16[1,128,2048]{2,1,0:T(8,128)(2,1)S(1)} copy-done((bf16[1,128,2048]{2,1,0:T(8,128)(2,1)S(1)}, bf16[1,128,2048]{2,1,0:T(8,128)(2,1)}, u32[]{:S(2)}) %copy-start.1) | copy-done | bytes 524312
  2.7 0.0 copy-start.2
  2.7 1.0 %copy-done.2 = bf16[128,2048]{1,0:T(8,128)(2,1)S(1)} copy-done((bf16[128,2048]{1,0:T(8,128)(2,1)S(1)}, bf16[128,2048]{1,0:T(8,128)(2,1)}, u32[]{:S(2)}) %copy-start.2) | copy-done | bytes 524312
  3.8 0.0 copy-start.3
  3.8 1.2 %copy-done.3 = bf16[2,512,512]{2,1,0:T(8,128)(2,1)S(1)} copy-done((bf16[2,512,512]{2,1,0:T(8,128)(2,1)S(1)}, bf16[2,512,512]{2,1,0:T(8,128)(2,1)}, u32[]{:S(2)}) %copy-start.3) | copy-done | bytes 1048600
  5.0 0.0 copy-start.4
  5.0 0.9 %copy-done.4 = f32[256,128]{1,0:T(8,128)S(1)} copy-done((f32[256,128]{1,0:T(8,128)S(1)}, f32[256,128]{1,0:T(8,128)}, u32[]{:S(2)}) %copy-start.4) | copy-done | bytes 131096
  5.9 65.4 %shard_map.68 = (bf16[128,2048]{1,0:T(8,128)(2,1)S(1)}, f32[128,1024]{1,0:T(8,128)S(1)}) custom-call(bf16[128,2048]{1,0:T(8,128)(2,1)S(1)} %bitcast.4, bf16[128,2048]{1,0:T(8,128)(2,1)S(1)} %bitcast.5, bf16[128,2048]{1,0:T(8,128)(2,1)S(1)} %copy-done.2, bf16[2,512,512]{2,1,0:T(8,128)(2,1)S(1)} %copy-done.3, f32[256,128]{1,0:T(8,128)S(1)} %copy-done.4), custom_call_target="tpu_custom_call" | custom-call | flops 9059696640 | bytes 6291456 | tf_op jit(solution)/shard_map/pallas_call | solution.py:437
  71.3 0.8 %copy.9 = bf16[1,128,2048]{2,1,0:T(8,128)(2,1)} copy(bf16[1,128,2048]{2,1,0:T(8,128)(2,1)S(1)} %bitcast.3) | data formatting | bytes 1048576
  72.1 0.8 %copy.10 = f32[128,1024]{1,0:T(8,128)} copy(f32[128,1024]{1,0:T(8,128)S(1)} %get-tuple-element.9) | data formatting | bytes 1048576
Async XLA Ops:
  0.6 1.0 %copy-start = (bf16[1,128,2048]{2,1,0:T(8,128)(2,1)S(1)}, bf16[1,128,2048]{2,1,0:T(8,128)(2,1)}, u32[]{:S(2)}) copy-start(bf16[1,128,2048]{2,1,0:T(8,128)(2,1)} %param.5) | copy-start | bytes 1572868
  1.7 1.0 %copy-start.1 = (bf16[1,128,2048]{2,1,0:T(8,128)(2,1)S(1)}, bf16[1,128,2048]{2,1,0:T(8,128)(2,1)}, u32[]{:S(2)}) copy-start(bf16[1,128,2048]{2,1,0:T(8,128)(2,1)} %param.6) | copy-start | bytes 1572868
  2.7 1.0 %copy-start.2 = (bf16[128,2048]{1,0:T(8,128)(2,1)S(1)}, bf16[128,2048]{1,0:T(8,128)(2,1)}, u32[]{:S(2)}) copy-start(bf16[128,2048]{1,0:T(8,128)(2,1)} %taps_ref.1) | copy-start | bytes 1572868
  3.8 1.2 %copy-start.3 = (bf16[2,512,512]{2,1,0:T(8,128)(2,1)S(1)}, bf16[2,512,512]{2,1,0:T(8,128)(2,1)}, u32[]{:S(2)}) copy-start(bf16[2,512,512]{2,1,0:T(8,128)(2,1)} %constant.4.clone.table_ref) | copy-start | bytes 3145732
  5.0 0.9 %copy-start.4 = (f32[256,128]{1,0:T(8,128)S(1)}, f32[256,128]{1,0:T(8,128)}, u32[]{:S(2)}) copy-start(f32[256,128]{1,0:T(8,128)} %constant.5.clone.columns_ref) | copy-start | bytes 393220
where the time goes:
time: 73.2 us; the launch traced here: 72.9 us
  Pallas kernels  65.4 us (89%)
  local copies, waits for them, and re-layouts  6.83 us (9%)
    pallas_call x1, Pallas kernels, fused(): pl.pallas_call(functools.partial(kernel, groups), out_shape=(jax.ShapeDty...  65.4 us
    unnamed x12, local copies, waits for them, and re-layouts  6.83 us

commit v1 on v0

--- a/solution.py
+++ b/solution.py
@@ -239,7 +239,7 @@
     inner_dft(table_ref, high_ref, low_ref, spec_ref)
 
 
-def correlate(left_ref, right_ref, twist_ref, table_ref, high_ref, low_ref, work_ref, store):
+def correlate(left_ref, right_ref, twist_ref, table_ref, high_ref, low_ref, work_ref, store, flush):
     @pl.loop(0, INNER // ROWS)
     def _(i):
         row = i * ROWS
@@ -255,8 +255,7 @@
 
     inner_dft(table_ref, high_ref, low_ref, work_ref)
 
-    @pl.loop(0, INNER // ROWS)
-    def _(i):
+    def finish(i):
         row = i * ROWS
         top = pl.ds(pl.multiple_of(row, ROWS), ROWS)
         bottom = pl.ds(pl.multiple_of(INNER + row, ROWS), ROWS)
@@ -270,14 +269,20 @@
         for q, value in enumerate(gather(z)):
             store(q * INNER + row, value)
 
+    steps = INNER // ROWS // 2
+    pl.loop(0, steps)(finish)
+    flush(0)
+    pl.loop(steps, 2 * steps)(finish)
+    flush(1)
+
 
 def kernel(
     groups,
     grad_ref,
     input_ref,
     taps_ref,
-    table_ref,
-    columns_ref,
+    table_hbm,
+    columns_hbm,
     grad_input_ref,
     filter_grad_ref,
     grad_in,
@@ -293,6 +298,9 @@
     back,
     partial,
     arrived,
+    table_ref,
+    columns_ref,
+    table_sem,
     send_sem,
     recv_sem,
     own_sem,
@@ -305,6 +313,11 @@
     group = lax.axis_index("dp")
     other = 1 - group
 
+    table_copy = pltpu.make_async_copy(table_hbm, table_ref, table_sem.at[0])
+    columns_copy = pltpu.make_async_copy(columns_hbm, columns_ref, table_sem.at[1])
+    columns_copy.start()
+    table_copy.start()
+
     barrier = pltpu.get_barrier_semaphore()
 
     @pl.loop(1, groups)
@@ -322,7 +335,7 @@
     def lanes_of(device):
         return pl.ds(pl.multiple_of(device * LANES, LANES), LANES)
 
-    outward = ((grad_ref, grad_in), (taps_ref, taps_in), (input_ref, input_in))
+    outward = ((grad_ref, grad_in), (input_ref, input_in), (taps_ref, taps_in))
 
     def copy_out(a, peer, dest_rows, recv_at):
         source, landing = outward[a]
@@ -364,8 +377,10 @@
 
         own_out(a).start()
 
+    columns_copy.wait()
     for i in range(2 * HALF):
         twist[i] = jnp.broadcast_to(columns_ref[:, i : i + 1], (INNER, LANES))
+    table_copy.wait()
 
     def wait_for(a):
         own_out(a).wait()
@@ -379,35 +394,52 @@
     wait_for(0)
     transform(grad_in, *shared, grad_spec)
     wait_for(1)
+    transform(input_in, *shared, input_spec)
+
+    def store_partial(row, value):
+        partial[pl.ds(pl.multiple_of(row, ROWS), ROWS), :] = value
+
+    def pair_copy(part, q):
+        rows = INNER // 2
+        at = q * INNER + part * rows
+        return pltpu.make_async_remote_copy(
+            src_ref=partial.at[pl.ds(pl.multiple_of(other * half + at, rows), rows), :],
+            dst_ref=arrived.at[pl.ds(at, rows), :],
+            send_sem=pair_send.at[part, q],
+            recv_sem=pair_recv.at[part, q],
+            device_id=(other, me),
+            device_id_type=MESH,
+        )
+
+    def flush_partial(part):
+        for q in range(HALF // 2):
+            pair_copy(part, q).start()
+
+    correlate(grad_spec, input_spec, *shared, work, store_partial, flush_partial)
+    wait_for(2)
     transform(taps_in, *shared, taps_spec)
 
     def store_back(row, value):
         back[pl.ds(pl.multiple_of(row, ROWS), ROWS), :] = value.astype(jnp.bfloat16)
 
-    correlate(grad_spec, taps_spec, *shared, work, store_back)
-
-    @pl.loop(1, groups)
-    def _(d):
-        copy_back(lax.rem(me + d, groups), me, me).start()
-
-    own_back().start()
-    wait_for(2)
-    transform(input_in, *shared, input_spec)
-
-    def store_partial(row, value):
-        partial[pl.ds(pl.multiple_of(row, ROWS), ROWS), :] = value
-
-    correlate(grad_spec, input_spec, *shared, work, store_partial)
-    pair = pltpu.make_async_remote_copy(
-        src_ref=partial.at[pl.ds(pl.multiple_of(other * half, half), half), :],
-        dst_ref=arrived,
-        send_sem=pair_send,
-        recv_sem=pair_recv,
-        device_id=(other, me),
-        device_id_type=MESH,
-    )
-    pair.start()
-    pair.wait()
+    def flush_back(part):
+        @pl.loop(0, groups // 2)
+        def _(d):
+            peer = lax.rem(me + 2 * d, groups) // 2 * 2 + part
+
+            @pl.when(peer != me)
+            def _():
+                copy_back(peer, me, me).start()
+
+            @pl.when(peer == me)
+            def _():
+                own_back().start()
+
+    correlate(grad_spec, taps_spec, *shared, work, store_back, flush_back)
+
+    for part in range(2):
+        for q in range(HALF // 2):
+            pair_copy(part, q).wait()
 
     for i in range(half // LANES):
         mine = partial[pl.ds(pl.multiple_of(group * half + i * LANES, LANES), LANES), :]
@@ -440,7 +472,7 @@
             jax.ShapeDtypeStruct((tokens, width), jnp.bfloat16),
             jax.ShapeDtypeStruct((LANES, length // 2), jnp.float32),
         ),
-        in_specs=[anywhere, anywhere, anywhere, vmem, vmem],
+        in_specs=[anywhere] * 5,
         out_specs=(anywhere, vmem),
         scratch_shapes=[
             landing,
@@ -456,14 +488,17 @@
             pltpu.VMEM((length, LANES), jnp.bfloat16),
             pltpu.VMEM((length, LANES), jnp.float32),
             pltpu.VMEM((length // 2, LANES), jnp.float32),
+            pltpu.VMEM((2, 2 * INNER, 2 * INNER), jnp.bfloat16),
+            pltpu.VMEM((INNER, LANES), jnp.float32),
+            pltpu.SemaphoreType.DMA((2,)),
             pltpu.SemaphoreType.DMA((4, groups)),
             pltpu.SemaphoreType.DMA((4, groups)),
             pltpu.SemaphoreType.DMA((4,)),
-            pltpu.SemaphoreType.DMA,
-            pltpu.SemaphoreType.DMA,
+            pltpu.SemaphoreType.DMA((2, HALF // 2)),
+            pltpu.SemaphoreType.DMA((2, HALF // 2)),
         ],
         compiler_params=pltpu.CompilerParams(
-            collective_id=0, has_side_effects=True, vmem_limit_bytes=40 * 1024 * 1024
+            collective_id=0, has_side_effects=True, vmem_limit_bytes=63 * 1024 * 1024
         ),
         cost_estimate=pl.CostEstimate(
             flops=5 * 3 * 2 * 512 * 512 * KEPT * LANES, bytes_accessed=6 << 20, transcendentals=0
@@ -485,7 +520,7 @@
         lax.axis_size("dp") == 2
         and groups * tokens == HALF * INNER
         and width == groups * LANES
-        and tokens % ROWS == 0
+        and 2 * tokens == INNER
     )
     return (fused if fits else local)(grad_output, conv_input, filter_taps)
 

time: 73.2 us -> 68 us (0.929)
  local copies, waits for them, and re-layouts: 6.83 us -> 2.74 us
  Pallas kernels: 65.4 us -> 64.2 us
    unnamed x12 -> x4, local copies, waits for them, and re-layouts: 6.83 us -> 2.74 us
    pallas_call x1, Pallas kernels: 65.4 us -> 64.2 us  [fused(): pl.pallas_call(functools.partial(kernel, groups), out_shape=(jax.ShapeDty...]
where the time goes in v1:
time: 68 us; the launch traced here: 67.6 us
  Pallas kernels  64.2 us (94%)
  local copies, waits for them, and re-layouts  2.74 us (4%)
    pallas_call x1, Pallas kernels, fused(): pl.pallas_call(functools.partial(kernel, groups), out_shape=(jax.ShapeDty...  64.2 us
    unnamed x4, local copies, waits for them, and re-layouts  2.74 us

profile of v1, /device:TPU:29, one launch (start us, length us, event | category | flops | bytes accessed | tf_op | source)
XLA Modules:
  0.0 67.6 jit_solution(8342374022785652548)
XLA Ops:
  0.6 64.2 %shard_map.68 = (bf16[128,2048]{1,0:T(8,128)(2,1)}, f32[128,1024]{1,0:T(8,128)}) custom-call(bf16[128,2048]{1,0:T(8,128)(2,1)} %bitcast.4, bf16[128,2048]{1,0:T(8,128)(2,1)} %bitcast.5, bf16[128,2048]{1,0:T(8,128)(2,1)} %taps_ref.1, bf16[2,512,512]{2,1,0:T(8,128)(2,1)} %constant.4.clone.table_hbm, f32[256,128]{1,0:T(8,128)} %constant.5.clone.columns_hbm), custom_call_target="tpu_custom_call" | custom-call | flops 9059696640 | bytes 6291456 | tf_op jit(solution)/shard_map/pallas_call | solution.py:469
  64.8 0.0 copy-start
  64.9 1.9 %copy.9 = bf16[1,128,2048]{2,1,0:T(8,128)(2,1)} copy(bf16[1,128,2048]{2,1,0:T(8,128)(2,1)} %bitcast.3) | data formatting | bytes 1048576
  66.8 0.0 copy-done
  66.8 0.8 %copy.10 = f32[128,1024]{1,0:T(8,128)} copy(f32[128,1024]{1,0:T(8,128)S(1)} %copy-done) | data formatting | bytes 1048576
Async XLA Ops:
  64.8 2.0 %copy-start = (f32[128,1024]{1,0:T(8,128)S(1)}, f32[128,1024]{1,0:T(8,128)}, u32[]{:S(2)}) copy-start(f32[128,1024]{1,0:T(8,128)} %get-tuple-element.9) | copy-start | bytes 1572868

commit v2 on v1

--- a/solution.py
+++ b/solution.py
@@ -369,13 +369,17 @@
             back.at[rows_of(me), :], grad_input_ref.at[:, lanes_of(me)], own_sem.at[3]
         )
 
-    for a in range(3):
-
+    def send(a):
         @pl.loop(1, groups)
         def _(d):
-            copy_out(a, lax.rem(me + d, groups), me, me).start()
-
+            peer = lax.rem(me + d, groups)
+            if a > 0:
+                copy_out(a - 1, peer, peer, peer).wait_send()
+            copy_out(a, peer, me, me).start()
+
+    for a in range(3):
         own_out(a).start()
+    send(0)
 
     columns_copy.wait()
     for i in range(2 * HALF):
@@ -391,8 +395,10 @@
             copy_out(a, peer, peer, peer).wait_recv()
 
     shared = (twist, table_ref, high, low)
+    send(1)
     wait_for(0)
     transform(grad_in, *shared, grad_spec)
+    send(2)
     wait_for(1)
     transform(input_in, *shared, input_spec)
 
@@ -453,8 +459,7 @@
     def _(d):
         peer = lax.rem(me + d, groups)
         copy_back(peer, peer, peer).wait()
-        for a in range(3):
-            copy_out(a, peer, peer, peer).wait_send()
+        copy_out(2, peer, peer, peer).wait_send()
 
 
 def fused(grad_output, conv_input, filter_taps):

time: 68 us -> 68.3 us (level)
  no operation moved by 1% of the time
where the time goes in v2:
time: 68.3 us; the launch traced here: 67.6 us
  Pallas kernels  64.2 us (94%)
  local copies, waits for them, and re-layouts  2.74 us (4%)
    pallas_call x1, Pallas kernels, fused(): pl.pallas_call(functools.partial(kernel, groups), out_shape=(jax.ShapeDty...  64.2 us
    unnamed x4, local copies, waits for them, and re-layouts  2.74 us

profile of v2, /device:TPU:29, one launch (start us, length us, event | category | flops | bytes accessed | tf_op | source)
XLA Modules:
  0.0 67.6 jit_solution(18232977145036956282)
XLA Ops:
  0.6 64.2 %shard_map.68 = (bf16[128,2048]{1,0:T(8,128)(2,1)}, f32[128,1024]{1,0:T(8,128)}) custom-call(bf16[128,2048]{1,0:T(8,128)(2,1)} %bitcast.4, bf16[128,2048]{1,0:T(8,128)(2,1)} %bitcast.5, bf16[128,2048]{1,0:T(8,128)(2,1)} %taps_ref.1, bf16[2,512,512]{2,1,0:T(8,128)(2,1)} %constant.4.clone.table_hbm, f32[256,128]{1,0:T(8,128)} %constant.5.clone.columns_hbm), custom_call_target="tpu_custom_call" | custom-call | flops 9059696640 | bytes 6291456 | tf_op jit(solution)/shard_map/pallas_call | solution.py:474
  64.8 0.0 copy-start
  64.8 1.9 %copy.9 = bf16[1,128,2048]{2,1,0:T(8,128)(2,1)} copy(bf16[1,128,2048]{2,1,0:T(8,128)(2,1)} %bitcast.3) | data formatting | bytes 1048576
  66.8 0.0 copy-done
  66.8 0.8 %copy.10 = f32[128,1024]{1,0:T(8,128)} copy(f32[128,1024]{1,0:T(8,128)S(1)} %copy-done) | data formatting | bytes 1048576
Async XLA Ops:
  64.8 2.0 %copy-start = (f32[128,1024]{1,0:T(8,128)S(1)}, f32[128,1024]{1,0:T(8,128)}, u32[]{:S(2)}) copy-start(f32[128,1024]{1,0:T(8,128)} %get-tuple-element.9) | copy-start | bytes 1572868

commit v3 on v1

--- a/solution.py
+++ b/solution.py
@@ -114,6 +114,7 @@
     phase = 2.0 * np.pi * (np.outer(index, index) % INNER) / INNER
     cos, sin = np.cos(phase), np.sin(phase)
     table = np.block([[cos, sin], [-sin, cos]]).astype(np.float32)
+    table = table.reshape(2, 2, INNER // 2, 2 * INNER).transpose(1, 0, 2, 3).reshape(table.shape)
     high = table.astype(jnp.bfloat16)
     low = (table - high.astype(np.float32)).astype(jnp.bfloat16)
     return np.stack([high, low])
@@ -197,13 +198,13 @@
     low_ref[at] = (value - high.astype(jnp.float32)).astype(jnp.bfloat16)
 
 
-def inner_dft(table_ref, high_ref, low_ref, out_ref):
+def inner_dft(table_ref, high_ref, low_ref, out_ref, rows):
     def block(at):
         high, low = high_ref[:, at], low_ref[:, at]
-        out_ref[:, at] = (
-            jnp.dot(table_ref[0], high, preferred_element_type=jnp.float32)
-            + jnp.dot(table_ref[0], low, preferred_element_type=jnp.float32)
-            + jnp.dot(table_ref[1], high, preferred_element_type=jnp.float32)
+        out_ref[rows, at] = (
+            jnp.dot(table_ref[0, rows, :], high, preferred_element_type=jnp.float32)
+            + jnp.dot(table_ref[0, rows, :], low, preferred_element_type=jnp.float32)
+            + jnp.dot(table_ref[1, rows, :], high, preferred_element_type=jnp.float32)
         )
 
     @pl.loop(0, HALF // 2)
@@ -236,44 +237,52 @@
             put_parts(high_ref, low_ref, row, r, re)
             put_parts(high_ref, low_ref, INNER + row, r, im)
 
-    inner_dft(table_ref, high_ref, low_ref, spec_ref)
+    inner_dft(table_ref, high_ref, low_ref, spec_ref, pl.ds(0, 2 * INNER))
 
 
 def correlate(left_ref, right_ref, twist_ref, table_ref, high_ref, low_ref, work_ref, store, flush):
-    @pl.loop(0, INNER // ROWS)
-    def _(i):
-        row = i * ROWS
-        top = pl.ds(pl.multiple_of(row, ROWS), ROWS)
-        bottom = pl.ds(pl.multiple_of(INNER + row, ROWS), ROWS)
-        for r in range(KEPT):
-            lanes = pl.ds(r * LANES, LANES)
-            scale = (1.0 if r in (0, HALF) else 2.0) / (RADIX * INNER)
-            lr, li = left_ref[top, lanes] * scale, left_ref[bottom, lanes] * scale
-            rr, ri = right_ref[top, lanes], right_ref[bottom, lanes]
-            put_parts(high_ref, low_ref, row, r, li * rr - lr * ri)
-            put_parts(high_ref, low_ref, INNER + row, r, lr * rr + li * ri)
-
-    inner_dft(table_ref, high_ref, low_ref, work_ref)
-
-    def finish(i):
-        row = i * ROWS
-        top = pl.ds(pl.multiple_of(row, ROWS), ROWS)
-        bottom = pl.ds(pl.multiple_of(INNER + row, ROWS), ROWS)
-        z = [work_ref[bottom, pl.ds(0, LANES)]]
-        for r in range(1, KEPT):
-            lanes = pl.ds(r * LANES, LANES)
-            im, re = work_ref[top, lanes], work_ref[bottom, lanes]
-            c, s = twist_ref[r - 1, top, :], twist_ref[HALF + r - 1, top, :]
-            z.append((re * c - im * s, re * s + im * c))
-        z[8] = z[8][0]
-        for q, value in enumerate(gather(z)):
-            store(q * INNER + row, value)
-
     steps = INNER // ROWS // 2
-    pl.loop(0, steps)(finish)
-    flush(0)
-    pl.loop(steps, 2 * steps)(finish)
-    flush(1)
+
+    def parts(part, i):
+        top = part * INNER + i * ROWS
+        return (
+            pl.ds(pl.multiple_of(top, ROWS), ROWS),
+            pl.ds(pl.multiple_of(top + INNER // 2, ROWS), ROWS),
+        )
+
+    for part in range(2):
+
+        @pl.loop(0, steps)
+        def _(i):
+            row = part * (INNER // 2) + i * ROWS
+            top, bottom = parts(part, i)
+            for r in range(KEPT):
+                lanes = pl.ds(r * LANES, LANES)
+                scale = (1.0 if r in (0, HALF) else 2.0) / (RADIX * INNER)
+                lr, li = left_ref[top, lanes] * scale, left_ref[bottom, lanes] * scale
+                rr, ri = right_ref[top, lanes], right_ref[bottom, lanes]
+                put_parts(high_ref, low_ref, row, r, li * rr - lr * ri)
+                put_parts(high_ref, low_ref, INNER + row, r, lr * rr + li * ri)
+
+    for part in range(2):
+        inner_dft(table_ref, high_ref, low_ref, work_ref, pl.ds(part * INNER, INNER))
+
+        @pl.loop(0, steps)
+        def _(i):
+            row = part * (INNER // 2) + i * ROWS
+            rows = pl.ds(pl.multiple_of(row, ROWS), ROWS)
+            top, bottom = parts(part, i)
+            z = [work_ref[bottom, pl.ds(0, LANES)]]
+            for r in range(1, KEPT):
+                lanes = pl.ds(r * LANES, LANES)
+                im, re = work_ref[top, lanes], work_ref[bottom, lanes]
+                c, s = twist_ref[r - 1, rows, :], twist_ref[HALF + r - 1, rows, :]
+                z.append((re * c - im * s, re * s + im * c))
+            z[8] = z[8][0]
+            for q, value in enumerate(gather(z)):
+                store(q * INNER + row, value)
+
+        flush(part)
 
 
 def kernel(
@@ -443,7 +452,7 @@
 
     for i in range(half // LANES):
         mine = partial[pl.ds(pl.multiple_of(group * half + i * LANES, LANES), LANES), :]
-        filter_grad_ref[:, i * LANES : (i + 1) * LANES] = jnp.transpose(
+        filter_grad_ref[i * LANES : (i + 1) * LANES, :] = (
             mine + arrived[i * LANES : (i + 1) * LANES, :]
         )
 
@@ -470,7 +479,7 @@
         functools.partial(kernel, groups),
         out_shape=(
             jax.ShapeDtypeStruct((tokens, width), jnp.bfloat16),
-            jax.ShapeDtypeStruct((LANES, length // 2), jnp.float32),
+            jax.ShapeDtypeStruct((length // 2, LANES), jnp.float32),
         ),
         in_specs=[anywhere] * 5,
         out_specs=(anywhere, vmem),
@@ -510,7 +519,7 @@
         jnp.asarray(inner_tables()),
         jnp.asarray(twist_columns()),
     )
-    return (grad_input[None], filter_grad)
+    return (grad_input[None], jnp.transpose(filter_grad))
 
 
 def any_size(grad_output, conv_input, filter_taps):

time: 68 us -> 68 us (level)
  no operation moved by 1% of the time
where the time goes in v3:
time: 68 us; the launch traced here: 67.6 us
  Pallas kernels  64 us (94%)
  local copies, waits for them, and re-layouts  2.89 us (4%)
    pallas_call x1, Pallas kernels, fused(): pl.pallas_call(functools.partial(kernel, groups), out_shape=(jax.ShapeDty...  64 us
    unnamed x4, local copies, waits for them, and re-layouts  2.89 us

profile of v3, /device:TPU:29, one launch (start us, length us, event | category | flops | bytes accessed | tf_op | source)
XLA Modules:
  0.0 67.6 jit_solution(6909966762656473844)
XLA Ops:
  0.6 64.0 %shard_map.68 = (bf16[128,2048]{1,0:T(8,128)(2,1)}, f32[1024,128]{1,0:T(8,128)}) custom-call(bf16[128,2048]{1,0:T(8,128)(2,1)} %bitcast.6, bf16[128,2048]{1,0:T(8,128)(2,1)} %bitcast.7, bf16[128,2048]{1,0:T(8,128)(2,1)} %taps_ref.1, bf16[2,512,512]{2,1,0:T(8,128)(2,1)} %constant.4.clone.table_hbm, f32[256,128]{1,0:T(8,128)} %constant.5.clone.columns_hbm), custom_call_target="tpu_custom_call" | custom-call | flops 9059696640 | bytes 6291456 | tf_op jit(solution)/shard_map/pallas_call | solution.py:478
  64.7 0.0 copy-start
  64.7 2.1 %copy.7 = f32[128,1024]{1,0:T(8,128)} copy(f32[128,1024]{0,1:T(8,128)} %bitcast.5) | data formatting | bytes 1048576
  66.8 0.0 copy-done
  66.8 0.8 %copy.9 = bf16[1,128,2048]{2,1,0:T(8,128)(2,1)} copy(bf16[1,128,2048]{2,1,0:T(8,128)(2,1)S(1)} %bitcast.4) | data formatting | bytes 1048576
Async XLA Ops:
  64.7 2.1 %copy-start = (bf16[128,2048]{1,0:T(8,128)(2,1)S(1)}, bf16[128,2048]{1,0:T(8,128)(2,1)}, u32[]{:S(2)}) copy-start(bf16[128,2048]{1,0:T(8,128)(2,1)} %get-tuple-element.4) | copy-start | bytes 1572868
